TPU v7x, 32 devices: a whole 2x2x4 slice. The times are simulated.
32 devices in a mesh: mom: 8 (over z, y), idx: 4 (over x, core).
Axes of the slice: x: 2, y: 2, z: 4, core: 2. Of those that a mesh axis runs over, the one named last changes fastest.
Arguments:
- vertex: bfloat16 [3, 256, 512, 512], P(None, 'mom', None, 'idx'), may hold values from -0.25 to 0.25
- formfactors: bfloat16 [2048, 512], replicated, may hold values from -6 to 6
- propagator: float32 [256], replicated, may hold values from -4 to 4
- loop_mom: int32 [2048], replicated, may hold values from 0 to 255
- bond_disp: int32 [8, 2], replicated, may hold values from 0 to 15
- proj_channel: int32 [3, 8, 4], replicated, may hold values from 0 to 2
- proj_bond: int32 [3, 8, 4], replicated, may hold values from 0 to 7
- proj_phase: int32 [3, 8, 4], replicated, may hold values from 0 to 3
Outputs:
- flow: float32 [3, 256, 512, 512], P(None, 'mom', None, 'idx')
All inputs are finite; a program needn't handle non-finite values.
Results may differ from a plain program's by a relative error of at most 0.005.
Values may be sent and summed in bfloat16 or wider, within the bound.
A program may use at most 192 MiB of HBM per device.

v0:
```python
import math

import jax
import jax.numpy as jnp
from jax import lax
from jax.sharding import PartitionSpec as P

MSIDE = 16


def momentum_sum(former, latter, signed):
    coord_x = (former // MSIDE + signed * (latter // MSIDE)) % MSIDE
    coord_y = (former % MSIDE + signed * (latter % MSIDE)) % MSIDE
    return coord_x * MSIDE + coord_y


def lookup(values, indices):
    hits = indices[..., None] == jnp.arange(values.shape[0], dtype=jnp.int32)
    return jnp.sum(jnp.where(hits, values, 0.0), axis=-1)


def loop_weights(propagator, loop_mom, momenta):
    pair = momentum_sum(momenta[:, None], loop_mom[None, :], -1)
    plus = momentum_sum(loop_mom[None, :], momenta[:, None], 1)
    minus = momentum_sum(loop_mom[None, :], momenta[:, None], -1)
    own = lookup(propagator, loop_mom)[None, :]
    return jnp.stack(
        [
            own * lookup(propagator, pair),
            own * lookup(propagator, plus),
            own * lookup(propagator, minus),
        ]
    )


def phase_table(bond_disp, momenta):
    coord_x = momenta // MSIDE
    coord_y = momenta % MSIDE
    turns = (bond_disp[:, 0:1] * coord_x[None, :] + bond_disp[:, 1:2] * coord_y[None, :]) % MSIDE
    angles = turns.astype(jnp.float32) * (2.0 * math.pi / MSIDE)
    return jnp.stack([jnp.cos(angles), -jnp.sin(angles)]).astype(jnp.bfloat16)


def mixing_tables(proj_channel, proj_bond, proj_phase):
    chan_hot = (proj_channel[..., None] == jnp.arange(3, dtype=jnp.int32)).astype(jnp.float32)
    bond_hot = (proj_bond[..., None] == jnp.arange(proj_bond.shape[1], dtype=jnp.int32)).astype(
        jnp.float32
    )
    direct = (proj_phase == 0).astype(jnp.float32) - (proj_phase == 2).astype(jnp.float32)
    crossed = (proj_phase == 3).astype(jnp.float32) - (proj_phase == 1).astype(jnp.float32)
    same = jnp.einsum(
        "xysu,xysv,xys->xyuv", chan_hot, bond_hot, direct, precision=lax.Precision.HIGHEST
    )
    swapped = jnp.einsum(
        "xysu,xysv,xys->xyuv", chan_hot, bond_hot, crossed, precision=lax.Precision.HIGHEST
    )
    return (same, swapped)


def mixing(table, values):
    return jnp.einsum("xyuv,iuvj->ixyj", table, values, precision=lax.Precision.HIGHEST)


def local(
    vertex, formfactors, propagator, loop_mom, bond_disp, proj_channel, proj_bond, proj_phase
):
    count_q = vertex.shape[1]
    q_ids = lax.axis_index("mom") * count_q + jnp.arange(count_q, dtype=jnp.int32)
    weights = loop_weights(propagator, loop_mom, q_ids)
    scale_nl = 1.0 / math.sqrt(formfactors.shape[0])
    loop_terms = jnp.einsum(
        "li,cqij->cqlj", formfactors, vertex, preferred_element_type=jnp.float32
    )
    weighted = (loop_terms * weights[..., None] * scale_nl).astype(jnp.bfloat16)
    kernel = jnp.einsum(
        "li,cqlj->cqij", formfactors, weighted, preferred_element_type=jnp.float32
    ).astype(jnp.bfloat16)
    increment = jnp.einsum(
        "cqia,cqaj->cqij",
        lax.all_gather(vertex, "idx", axis=3, tiled=True),
        kernel,
        preferred_element_type=jnp.float32,
    )
    increment_b = increment.astype(jnp.bfloat16)
    inv_side = 1.0 / MSIDE
    back_scale = 1.0 / math.sqrt(bond_disp.shape[0] * proj_channel.shape[2])
    same, swapped = mixing_tables(proj_channel, proj_bond, proj_phase)
    phases_own = phase_table(bond_disp, q_ids)
    bond_terms = lax.psum_scatter(
        jnp.einsum("pbq,cqij->icpbj", phases_own, increment_b, preferred_element_type=jnp.float32)
        * inv_side,
        "mom",
        scatter_dimension=0,
        tiled=True,
    )
    real_part = bond_terms[:, :, 0]
    imag_part = bond_terms[:, :, 1]
    proj_real = mixing(same, real_part) + mixing(swapped, imag_part)
    proj_imag = mixing(same, imag_part) - mixing(swapped, real_part)
    projected = jnp.stack([proj_real, proj_imag], axis=2).astype(jnp.bfloat16)
    returned = (
        jnp.einsum(
            "pbq,icpbj->cqij",
            phases_own,
            lax.all_gather(projected, "mom", axis=0, tiled=True),
            preferred_element_type=jnp.float32,
        )
        * back_scale
    )
    return increment + returned


def solution(mesh):
    in_specs = (P(None, "mom", None, "idx"), P(), P(), P(), P(), P(), P(), P())
    out_specs = P(None, "mom", None, "idx")
    return jax.shard_map(local, mesh=mesh, in_specs=in_specs, out_specs=out_specs, check_vma=False)
```

profile of v0, /device:TPU:0, one launch (start us, length us, event | category | flops | bytes accessed | tf_op | source)
XLA Modules:
  0.0 840.0 jit_solution(10795974494515816952)
XLA Ops:
  6.6 0.7 all-gather.3.cloned.1.call-update
  7.4 0.7 select_reduce_fusion.3
  8.2 0.1 cosine_convert_fusion
  8.3 0.7 fusion.23
  9.0 55.3 %select_reduce_fusion.2 = (f32[32,2048]{1,0:T(8,128)S(1)}, f32[32,2048]{1,0:T(8,128)S(1)}, f32[32,2048]{1,0:T(8,128)S(1)}) fusion(f32[256]{0:T(256)S(1)} %copy-done.6, s32[32,2048]{1,0:T(8,128)S(1)} %get-tuple-element.23, s32[32,2048]{1,0:T(8,128)S(1)} %get-tuple-element.11, s32[32,2048]{1,0:T(8,128)S(1)} %get-tuple-element.10), kind=kLoop, calls=%fused_computation.5 | loop fusion | flops 150798336 | bytes 1573888 | tf_op jit(solution)/shard_map/reduce_sum | solution.py:19
  64.5 35.7 %multiply_convert_fusion = bf16[3,32,128,2048]{3,2,1,0:T(8,128)(2,1)} fusion(bf16[3,32,512,128]{3,2,1,0:T(8,128)(2,1)} %param.8, f32[3,32,2048]{2,1,0:T(8,128)S(1)} %pad_maximum_fusion, bf16[2048,512]{1,0:T(8,128)(2,1)S(1)} %copy-done), kind=kOutput, calls=%fused_computation | convolution fusion | flops 25845301248 | bytes 65798144 | tf_op jit(solution)/shard_map/li,cqij->cqlj/dot_general | solution.py:71
  100.1 215.4 %all-gather.3.cloned.1.call-done = bf16[3,32,512,512]{3,2,1,0:T(8,128)(2,1)} async-done(((bf16[3,32,512,128]{3,2,1,0:T(8,128)(2,1)}), bf16[3,32,512,512]{3,2,1,0:T(8,128)(2,1)}) %all-gather.3.cloned.1.call-update) | async-done | bytes 50331664 | tf_op jit(solution)/shard_map/all_gather | solution.py:80
  315.5 50.7 %fusion.3 = f32[3,32,128,512]{3,2,1,0:T(8,128)} fusion(bf16[3,32,512,512]{3,2,1,0:T(8,128)(2,1)} %all-gather.3.cloned.1.call-done, bf16[3,32,128,2048]{3,2,1,0:T(8,128)(2,1)} %multiply_convert_fusion, bf16[2048,512]{1,0:T(8,128)(2,1)S(1)} %copy-done), kind=kOutput, calls=%fused_computation.14 | convolution fusion | flops 32218546176 | bytes 127926272 | tf_op jit(solution)/shard_map/cqia,cqaj->cqij/dot_general | solution.py:78
  366.2 13.3 %fusion.2 = bf16[3,32,512,128,1]{2,3,1,0,4:T(8,128)(2,1)} fusion(f32[3,32,128,512]{3,2,1,0:T(8,128)} %fusion.3), kind=kLoop, calls=%fused_computation.11 | loop fusion | flops 6291456 | bytes 37748736 | tf_op jit(solution)/shard_map/convert_element_type | solution.py:84
  379.5 17.5 %copy.56 = bf16[3,32,512,128,1]{3,1,4,2,0:T(8,128)(2,1)} copy(bf16[3,32,512,128,1]{2,3,1,0,4:T(8,128)(2,1)} %fusion.2) | data formatting | bytes 25165824 | tf_op jit(solution)/shard_map/convert_element_type | solution.py:84
  397.0 10.8 %multiply_bitcast_fusion = f32[512,3,2,8,128]{4,3,2,0,1:T(8,128)} fusion(bf16[3,32,512,128,1]{3,1,4,2,0:T(8,128)(2,1)} %copy.56, bf16[1,8,32]{2,1,0:T(8,128)(2,1)S(1)} %get-tuple-element.22, bf16[1,8,32]{2,1,0:T(8,128)(2,1)S(1)} %get-tuple-element.21), kind=kOutput, calls=%fused_computation.13 | convolution fusion | flops 204474368 | bytes 25166848 | tf_op jit(solution)/shard_map/pbq,cqij->icpbj/dot_general | solution.py:90
  407.8 9.9 %copy.71 = f32[512,3,2,8,128]{4,3,2,1,0:T(8,128)} copy(f32[512,3,2,8,128]{4,3,2,0,1:T(8,128)} %multiply_bitcast_fusion) | data formatting | bytes 25165824
  417.7 14.9 %copy.95 = f32[64,8,48,128]{3,1,2,0:T(8,128)} copy(f32[64,8,48,128]{3,2,1,0:T(8,128)} %bitcast.130) | data formatting | bytes 25165824
  432.6 0.3 all-gather.5.cloned.1.call-start
  432.9 0.4 copy-done.3
  433.3 0.1 copy.47
  433.4 0.1 copy.42
  433.5 0.1 copy.43
  433.7 0.3 fusion.30
  434.0 0.3 fusion.32
  434.3 205.9 %reduce-scatter.5.cloned.1.call-done = f32[64,6144]{1,0:T(8,128)} async-done(((f32[512,6144]{1,0:T(8,128)}), f32[64,6144]{1,0:T(8,128)}) %reduce-scatter.5.cloned.1.call-update) | async-done | bytes 1572880
  640.1 1.7 copy.77
  641.8 0.8 convolution_bitcast_fusion.3
  642.7 0.8 convolution_bitcast_fusion.1
  643.5 0.8 fusion.16
  644.3 0.8 fusion.17
  645.2 1.0 pad_maximum_fusion.1
  646.1 98.3 %all-gather.5.cloned.1.call-done = bf16[512,3,2,8,128]{4,3,1,0,2:T(8,128)(2,1)} async-done(((bf16[64,3,2,8,128]{4,3,1,0,2:T(8,128)(2,1)}), bf16[512,3,2,8,128]{4,3,1,0,2:T(8,128)(2,1)}) %all-gather.5.cloned.1.call-update) | async-done | bytes 6291472 | tf_op jit(solution)/shard_map/all_gather | solution.py:105
  744.4 14.5 %convolution_bitcast_fusion = f32[512,3,128,32]{2,3,1,0:T(8,128)} fusion(bf16[512,3,2,8,128]{4,3,1,0,2:T(8,128)(2,1)} %all-gather.5.cloned.1.call-done, bf16[1,8,32]{2,1,0:T(8,128)(2,1)S(1)} %get-tuple-element.22, bf16[1,8,32]{2,1,0:T(8,128)(2,1)S(1)} %get-tuple-element.21), kind=kOutput, calls=%fused_computation.16 | convolution fusion | flops 201327104 | bytes 31458304 | tf_op jit(solution)/shard_map/pbq,icpbj->cqij/dot_general | solution.py:102
  759.0 24.8 %copy.52 = f32[512,3,128,32]{0,2,3,1:T(8,128)} copy(f32[512,3,128,32]{2,3,1,0:T(8,128)} %convolution_bitcast_fusion) | data formatting | bytes 50331648 | tf_op jit(solution)/shard_map/pbq,icpbj->cqij/dot_general | solution.py:102
  783.8 24.8 %bitcast_add_fusion = f32[3,32,512,128]{2,3,1,0:T(8,128)} fusion(f32[3,32,128,512]{3,2,1,0:T(8,128)} %fusion.3, f32[512,3,128,32]{0,2,3,1:T(8,128)} %copy.52), kind=kLoop, calls=%fused_computation.9 | loop fusion | flops 12582912 | bytes 75497472 | tf_op jit(solution)/shard_map/add | solution.py:110
  808.6 24.8 %copy.53 = f32[3,32,512,128]{3,2,1,0:T(8,128)} copy(f32[3,32,512,128]{2,3,1,0:T(8,128)} %bitcast_add_fusion) | data formatting | bytes 50331648 | tf_op jit(solution)/shard_map/add | solution.py:110
  (27 shorter events, 0.4 us)
Async XLA Ops:
  6.5 57.9 %copy-start = (bf16[2048,512]{1,0:T(8,128)(2,1)S(1)}, bf16[2048,512]{1,0:T(8,128)(2,1)}, u32[]{:S(2)}) copy-start(bf16[2048,512]{1,0:T(8,128)(2,1)} %param.9) | copy-start | bytes 6291460
  6.5 0.8 copy-start.2
  6.5 0.8 copy-start.6
  6.5 1.6 copy-start.7
  6.5 309.0 %all-gather.3.cloned.1.call-start = ((), (), s32[]{:S(2)}) async-start(), calls=%async_computation.1 | async-start | bytes 62914560 | tf_op jit(solution)/shard_map/all_gather | solution.py:80
  7.3 632.9 %reduce-scatter.5.cloned.1.call-start = ((), (), s32[]{:S(2)}) async-start(), calls=%async_computation.3 | async-start | bytes 14155776
  432.6 0.7 copy-start.3
  432.6 0.8 copy-start.4
  432.6 0.9 copy-start.5
  432.6 311.8 %all-gather.5.cloned.1.call-start = ((), (), s32[]{:S(2)}) async-start(), calls=%async_computation.2 | async-start | bytes 7077888 | tf_op jit(solution)/shard_map/all_gather | solution.py:105
  808.6 24.8 %copy-start.1 = (bf16[2048,512]{1,0:T(8,128)(2,1)S(1)}, bf16[2048,512]{1,0:T(8,128)(2,1)}, u32[]{:S(2)}) copy-start(bf16[2048,512]{1,0:T(8,128)(2,1)} %param.9) | copy-start | bytes 6291460
Sparse Core Ops, SparseCore 0:
  8.9 306.5 all-gather.2
  432.8 207.3 reduce-scatter.4
  646.3 98.1 all-gather.4
where the time goes:
time: 841 us; the launch traced here: 840 us
  waiting for transfers between devices  520 us (62%)
  matrix products  116 us (14%)
  other arithmetic  96.1 us (11%)
  local copies, waits for them, and re-layouts  94.5 us (11%)
  between operations  13.3 us (2%)
    all_gather x1, waiting for transfers between devices, local(): lax.all_gather(vertex, 'idx', axis=3, tiled=True)  215 us
    unnamed x4, waiting for transfers between devices  207 us
    all_gather x1, waiting for transfers between devices, local(): lax.all_gather(projected, 'mom', axis=0, tiled=True)  98.3 us
    reduce_sum x2, other arithmetic, lookup(): return jnp.sum(jnp.where(hits, values, 0.0), axis=-1)  56 us
    dot_general x1, matrix products, local(): jnp.einsum('cqia,cqaj->cqij', lax.all_gather(vertex, 'idx', axis=3, tiled...  50.7 us
    dot_general x1, matrix products, local(): jnp.einsum('li,cqij->cqlj', formfactors, vertex, preferred_element_type=j...  35.7 us
    unnamed x21, local copies, waits for them, and re-layouts  27.1 us
    dot_general x1, local copies, waits for them, and re-layouts, local(): jnp.einsum('pbq,icpbj->cqij', phases_own, lax.all_gather(projected, 'mom'...  24.8 us
  transfers between devices with their start and end apart: 3, of which 3 were waited for; matrix products, arithmetic and copies ran while one was open for 11% of the time, Pallas kernels for 0%

commit v1 on v0

v1 whole, which is shorter than its diff:
```python
import functools
import math

import jax
import jax.numpy as jnp
from jax import lax
from jax.experimental import pallas as pl
from jax.experimental.pallas import tpu as pltpu
from jax.sharding import PartitionSpec as P

MSIDE = 16
VMEM = 56 * 1024 * 1024
GROUP = 16
DEPTH = 2
CHUNKS = (4, 4, 4, 2, 2)


def momentum_sum(former, latter, signed):
    coord_x = (former // MSIDE + signed * (latter // MSIDE)) % MSIDE
    coord_y = (former % MSIDE + signed * (latter % MSIDE)) % MSIDE
    return coord_x * MSIDE + coord_y


def lookup(values, indices):
    hits = indices[..., None] == jnp.arange(values.shape[0], dtype=jnp.int32)
    return jnp.sum(jnp.where(hits, values, 0.0), axis=-1)


def loop_weights(propagator, loop_mom, momenta):
    every = jnp.arange(propagator.shape[0], dtype=jnp.int32)
    pair = momentum_sum(momenta[:, None], every[None, :], -1)
    plus = momentum_sum(every[None, :], momenta[:, None], 1)
    minus = momentum_sum(every[None, :], momenta[:, None], -1)
    table = propagator * lookup(propagator, jnp.stack([pair, plus, minus]))
    hits = (every[:, None] == loop_mom[None, :]).astype(jnp.float32)
    return jnp.einsum("cqk,kl->cql", table, hits, precision=lax.Precision.HIGHEST)


def phase_table(bond_disp, momenta):
    coord_x = momenta // MSIDE
    coord_y = momenta % MSIDE
    turns = (bond_disp[:, 0:1] * coord_x[None, :] + bond_disp[:, 1:2] * coord_y[None, :]) % MSIDE
    angles = turns.astype(jnp.float32) * (2.0 * math.pi / MSIDE)
    return jnp.stack([jnp.cos(angles), -jnp.sin(angles)]).astype(jnp.bfloat16)


def mixing_tables(proj_channel, proj_bond, proj_phase):
    chan_hot = (proj_channel[..., None] == jnp.arange(3, dtype=jnp.int32)).astype(jnp.float32)
    bond_hot = (proj_bond[..., None] == jnp.arange(proj_bond.shape[1], dtype=jnp.int32)).astype(
        jnp.float32
    )
    direct = (proj_phase == 0).astype(jnp.float32) - (proj_phase == 2).astype(jnp.float32)
    crossed = (proj_phase == 3).astype(jnp.float32) - (proj_phase == 1).astype(jnp.float32)
    same = jnp.einsum(
        "xysu,xysv,xys->xyuv", chan_hot, bond_hot, direct, precision=lax.Precision.HIGHEST
    )
    swapped = jnp.einsum(
        "xysu,xysv,xys->xyuv", chan_hot, bond_hot, crossed, precision=lax.Precision.HIGHEST
    )
    return (same, swapped)


def kernel_body(v_ref, w_ref, ft_ref, ff_ref, out_ref, acc_ref):
    count = v_ref.shape[1]
    width = v_ref.shape[3]
    turned = jnp.concatenate([v_ref[0, q].T for q in range(count)], axis=0)
    step = ff_ref.shape[0] // 4
    acc_ref[...] = jnp.zeros_like(acc_ref)

    def part(index, carry):
        at = pl.ds(pl.multiple_of(index * step, step), step)
        terms = jnp.dot(turned, ft_ref[:, at], preferred_element_type=jnp.float32)
        weighted = terms.reshape(count, width, step) * w_ref[0, 0, :, at][:, None, :]
        weighted = weighted.reshape(count * width, step).astype(jnp.bfloat16)
        acc_ref[...] += jnp.dot(weighted, ff_ref[at, :], preferred_element_type=jnp.float32)
        return carry

    lax.fori_loop(0, 4, part, 0)
    out_ref[0] = acc_ref[...].astype(jnp.bfloat16).reshape(count, width, -1)


def bubble(channel, vertex, weights, forms_t, forms):
    _, count_q, rows, width = vertex.shape
    loops = forms.shape[0]
    block = math.gcd(count_q, 4)
    weights = weights.reshape(weights.shape[0], count_q // block, block, loops)
    return pl.pallas_call(
        kernel_body,
        grid=(count_q // block,),
        in_specs=[
            pl.BlockSpec((1, block, rows, width), lambda s: (channel, s, 0, 0)),
            pl.BlockSpec((1, 1, block, loops), lambda s: (channel, s, 0, 0)),
            pl.BlockSpec(forms_t.shape, lambda s: (0, 0)),
            pl.BlockSpec(forms.shape, lambda s: (0, 0)),
        ],
        out_specs=pl.BlockSpec((1, block, width, rows), lambda s: (0, s, 0, 0)),
        out_shape=jax.ShapeDtypeStruct((1, count_q, width, rows), jnp.bfloat16),
        scratch_shapes=[pltpu.VMEM((block * width, rows), jnp.float32)],
        compiler_params=pltpu.CompilerParams(vmem_limit_bytes=VMEM),
        cost_estimate=pl.CostEstimate(
            flops=4 * count_q * rows * width * loops,
            bytes_accessed=4 * count_q * rows * width,
            transcendentals=0,
        ),
    )(vertex, weights, forms_t, forms)


def step_body(slots, *refs):
    panels = refs[:slots]
    kernels = refs[slots : slots + 3]
    there_ref, inc_ref, bond_ref = refs[slots + 3 :]
    channel = pl.program_id(0)
    count_q, rows, width = inc_ref.shape[1:]
    for choice in range(3):

        @pl.when(channel == choice)
        def _():
            def one(q, carry):
                left = jnp.concatenate([panel[0, q] for panel in panels], axis=1)
                product = lax.dot_general(
                    left,
                    kernels[choice][0, q],
                    (((1,), (1,)), ((), ())),
                    preferred_element_type=jnp.float32,
                )
                inc_ref[0, q] = product.astype(jnp.bfloat16)
                return carry

            lax.fori_loop(0, count_q, one, 0, unroll=4)

    for start in range(0, rows, GROUP):
        piece = inc_ref[0, :, start : start + GROUP, :].reshape(count_q * GROUP, width)
        terms = jnp.dot(there_ref[...], piece, preferred_element_type=jnp.float32)
        bond_ref[0, :, start : start + GROUP, :] = terms.astype(jnp.bfloat16).reshape(
            -1, GROUP, width
        )


def increments(first, size, vertex, others, kernels, there):
    chans, count_q, rows_all, width = vertex.shape
    slots = 1 + len(others)
    terms = there.shape[0] // GROUP
    block = math.gcd(math.gcd(first, size), 128)
    lead = first // block
    kernel_spec = pl.BlockSpec(
        (1, count_q, width, rows_all), lambda c, s: (0, 0, 0, 0), pipeline_mode=pl.Buffered(1)
    )
    return pl.pallas_call(
        functools.partial(step_body, slots),
        grid=(chans, size // block),
        in_specs=[pl.BlockSpec((1, count_q, block, width), lambda c, s: (c, 0, s + lead, 0))]
        + [pl.BlockSpec((1, count_q, block, width), lambda c, s: (c, 0, s, 0))] * len(others)
        + [kernel_spec] * 3
        + [pl.BlockSpec(there.shape, lambda c, s: (0, 0))],
        out_specs=[
            pl.BlockSpec((1, count_q, block, width), lambda c, s: (c, 0, s, 0)),
            pl.BlockSpec((1, terms, block, width), lambda c, s: (c, 0, s, 0)),
        ],
        out_shape=[
            jax.ShapeDtypeStruct((chans, count_q, size, width), jnp.bfloat16),
            jax.ShapeDtypeStruct((chans, terms, size, width), jnp.bfloat16),
        ],
        compiler_params=pltpu.CompilerParams(vmem_limit_bytes=VMEM),
        cost_estimate=pl.CostEstimate(
            flops=8 * chans * count_q * rows_all * width * size,
            bytes_accessed=2 * chans * count_q * width * (rows_all + size * (slots + 1)),
            transcendentals=0,
        ),
    )(vertex, *others, *kernels, there)


def flow_body(scale, *refs):
    inc_ref, proj_ref, back_ref = refs[:3]
    out_ref = refs[-1]
    count_q, rows, width = inc_ref.shape[1:]
    terms = proj_ref.shape[1]
    for start in range(0, rows, GROUP):
        at = slice(start, start + GROUP)
        piece = proj_ref[0, :, at, :].reshape(terms * GROUP, width)
        back = jnp.dot(back_ref[...], piece, preferred_element_type=jnp.float32) * scale
        out_ref[0, :, at, :] = inc_ref[0, :, at, :].astype(jnp.float32) + back.reshape(
            count_q, GROUP, width
        )


def finish(first, flow, shape, inc, projected, back, scale):
    chans, count_q, size, width = inc.shape
    terms = projected.shape[1]
    block = math.gcd(math.gcd(first, size), 64)
    lead = first // block
    extra = [] if flow is None else [flow]
    return pl.pallas_call(
        functools.partial(flow_body, scale),
        grid=(chans, size // block),
        in_specs=[
            pl.BlockSpec((1, count_q, block, width), lambda c, s: (c, 0, s, 0)),
            pl.BlockSpec((1, terms, block, width), lambda c, s: (c, 0, s, 0)),
            pl.BlockSpec(back.shape, lambda c, s: (0, 0)),
        ]
        + [pl.BlockSpec(memory_space=pl.ANY)] * len(extra),
        out_specs=pl.BlockSpec((1, count_q, block, width), lambda c, s: (c, 0, s + lead, 0)),
        out_shape=jax.ShapeDtypeStruct(shape, jnp.float32),
        input_output_aliases={3: 0} if extra else {},
        compiler_params=pltpu.CompilerParams(vmem_limit_bytes=VMEM),
        cost_estimate=pl.CostEstimate(
            flops=2 * chans * count_q * size * width * terms * GROUP,
            bytes_accessed=6 * chans * count_q * size * width,
            transcendentals=0,
        ),
    )(inc, projected, back, *extra)


def swap(values, axis, count, bit):
    return lax.ppermute(values, axis, [(d, d ^ bit) for d in range(count)])


def bits_of(count):
    return [1 << k for k in range(count.bit_length() - 1)]


def scatter_sum(values, count):
    me = lax.axis_index("mom")
    for bit in bits_of(count):
        half = values.shape[2] // 2
        side = (me // bit) % 2
        mine = lax.dynamic_slice_in_dim(values, side * half, half, 2)
        theirs = lax.dynamic_slice_in_dim(values, (1 - side) * half, half, 2)
        got = swap(theirs, "mom", count, bit)
        total = mine.astype(jnp.float32) + got.astype(jnp.float32)
        values = total if bit * 2 == count else total.astype(jnp.bfloat16)
    return values.astype(jnp.float32)


def gather_rows(values, count):
    me = lax.axis_index("mom")
    for bit in reversed(bits_of(count)):
        side = (me // bit) % 2
        got = swap(values, "mom", count, bit)
        values = jnp.where(
            side == 0,
            jnp.concatenate([values, got], axis=2),
            jnp.concatenate([got, values], axis=2),
        )
    return values


def local(
    count_mom,
    count_idx,
    vertex,
    formfactors,
    propagator,
    loop_mom,
    bond_disp,
    proj_channel,
    proj_bond,
    proj_phase,
):
    chans, count_q, rows, width = vertex.shape
    parts = sum(CHUNKS)
    sizes = [rows * c // parts for c in CHUNKS]
    firsts = [sum(sizes[:k]) for k in range(len(sizes))]

    far = count_idx // 2
    held = []
    for k, (first, size) in enumerate(zip(firsts, sizes)):
        own = vertex[:, :, first : first + size, :]
        if k >= DEPTH:
            own, held[k - DEPTH][far] = lax.optimization_barrier((own, held[k - DEPTH][far]))
        slots = {0: own}
        for bit in reversed(bits_of(count_idx)):
            for slot in list(slots):
                slots[slot ^ bit] = swap(slots[slot], "idx", count_idx, bit)
        held.append(slots)

    q_ids = lax.axis_index("mom") * count_q + jnp.arange(count_q, dtype=jnp.int32)
    weights = loop_weights(propagator, loop_mom, q_ids) * (1.0 / math.sqrt(formfactors.shape[0]))
    me = lax.axis_index("idx")
    forms = jnp.concatenate(
        [
            lax.dynamic_slice_in_dim(formfactors, (me ^ slot) * width, width, 1)
            for slot in range(count_idx)
        ],
        axis=1,
    )
    forms_t = formfactors.T
    kernels = [bubble(c, vertex, weights, forms_t, forms) for c in range(chans)]

    bonds = bond_disp.shape[0]
    phases = phase_table(bond_disp, q_ids).reshape(2 * bonds, count_q)
    eye = jnp.eye(GROUP, dtype=jnp.bfloat16)
    there = jnp.einsum("tq,rs->trqs", phases * (1.0 / MSIDE), eye)
    there = there.astype(jnp.bfloat16).reshape(2 * bonds * GROUP, count_q * GROUP)
    back = jnp.einsum("tq,rs->qrts", phases, eye)
    back = back.astype(jnp.bfloat16).reshape(count_q * GROUP, 2 * bonds * GROUP)
    scale = 1.0 / math.sqrt(bonds * proj_channel.shape[2])
    same, swapped = mixing_tables(proj_channel, proj_bond, proj_phase)
    table = jnp.stack(
        [jnp.stack([same, swapped], axis=3), jnp.stack([-swapped, same], axis=3)], axis=1
    ).reshape(chans * 2 * bonds, chans * 2 * bonds)

    flow = None
    for first, size, slots in zip(firsts, sizes, held):
        others = [slots[slot] for slot in range(1, count_idx)]
        inc, bond = increments(first, size, vertex, others, kernels, there)
        summed = scatter_sum(bond, count_mom)
        mixed = jnp.einsum(
            "xk,krj->xrj",
            table,
            summed.reshape(table.shape[0], -1, width),
            precision=lax.Precision.HIGHEST,
        )
        projected = gather_rows(mixed.astype(jnp.bfloat16).reshape(summed.shape), count_mom)
        flow = finish(first, flow, vertex.shape, inc, projected, back, scale)
    return flow


def solution(mesh):
    in_specs = (P(None, "mom", None, "idx"), P(), P(), P(), P(), P(), P(), P())
    out_specs = P(None, "mom", None, "idx")
    body = functools.partial(local, mesh.shape["mom"], mesh.shape["idx"])
    return jax.shard_map(body, mesh=mesh, in_specs=in_specs, out_specs=out_specs, check_vma=False)
```

time: 841 us -> 502 us (0.60)
  waiting for transfers between devices: 520 us -> 177 us
  Pallas kernels: 0 us -> 196 us
  matrix products: 116 us -> 3.85 us
  other arithmetic: 96.1 us -> 38.1 us
  local copies, waits for them, and re-layouts: 94.5 us -> 38.9 us
  starting transfers between devices: 0.33 us -> 46.8 us
  between operations: 13.3 us -> 0.74 us
    all_gather x2 -> x0, waiting for transfers between devices: 314 us -> none  [the longest x1 215 us: local(): lax.all_gather(vertex, 'idx', axis=3, tiled=True)]
    unnamed x4 -> x0, waiting for transfers between devices: 207 us -> none
    pallas_call x0 -> x13, Pallas kernels: none -> 196 us  [the longest x3 85.4 us: bubble(): pl.pallas_call(kernel_body, grid=(count_q // block,), in_specs=[pl.BlockS...]
    ppermute x0 -> x45, waiting for transfers between devices: none -> 177 us  [swap(): return lax.ppermute(values, axis, [(d, d ^ bit) for d in range(count)])]
    dot_general x8 -> x6, matrix products: 115 us -> 3.28 us  [the longest x5 2.4 us: local(): jnp.einsum('xk,krj->xrj', table, summed.reshape(table.shape[0], -1, width...]
    reduce_sum x2 -> x1, other arithmetic: 56 us -> 8.38 us  [lookup(): return jnp.sum(jnp.where(hits, values, 0.0), axis=-1)]
    ppermute x0 -> x45, starting transfers between devices: none -> 46.8 us  [swap(): return lax.ppermute(values, axis, [(d, d ^ bit) for d in range(count)])]
    dot_general x1 -> x0, local copies, waits for them, and re-layouts: 24.8 us -> none  [local(): jnp.einsum('pbq,icpbj->cqij', phases_own, lax.all_gather(projected, 'mom'...]
  transfers between devices with their start and end apart: 3 -> 45, of which waited for: 3 -> 14; matrix products, arithmetic and copies ran while one was open for 11% -> 14% of each run, Pallas kernels for 0% -> 36%
where the time goes in v1:
time: 502 us; the launch traced here: 501 us
  Pallas kernels  196 us (39%)
  waiting for transfers between devices  177 us (35%)
  starting transfers between devices  46.8 us (9%)
  local copies, waits for them, and re-layouts  38.9 us (8%)
  other arithmetic  38.1 us (8%)
    ppermute x45, waiting for transfers between devices, swap(): return lax.ppermute(values, axis, [(d, d ^ bit) for d in range(count)])  177 us
    pallas_call x3, Pallas kernels, bubble(): pl.pallas_call(kernel_body, grid=(count_q // block,), in_specs=[pl.BlockS...  85.4 us
    pallas_call x5, Pallas kernels, increments(): pl.pallas_call(functools.partial(step_body, slots), grid=(chans, size //...  78.5 us
    ppermute x45, starting transfers between devices, swap(): return lax.ppermute(values, axis, [(d, d ^ bit) for d in range(count)])  46.8 us
    pallas_call x5, Pallas kernels, finish(): pl.pallas_call(functools.partial(flow_body, scale), grid=(chans, size //...  31.8 us
    select_n x15, other arithmetic, gather_rows(): jnp.where(side == 0, jnp.concatenate([values, got], axis=2), jnp.concaten...  22.2 us
    slice x2, local copies, waits for them, and re-layouts, local(): own = vertex[:, :, first:first + size, :]  12.9 us
  transfers between devices with their start and end apart: 45, of which 14 were waited for; matrix products, arithmetic and copies ran while one was open for 14% of the time, Pallas kernels for 36%

profile of v1, /device:TPU:0, one launch (start us, length us, event | category | flops | bytes accessed | tf_op | source)
XLA Modules:
  0.0 500.9 jit_solution(10006971987152296828)
XLA Ops:
  0.0 8.3 %fusion.41 = (bf16[3,32,128,128]{3,2,1,0:T(8,128)(2,1)}, bf16[3,32,128,128]{3,2,1,0:T(8,128)(2,1)}, bf16[3,32,128,128]{3,2,1,0:T(8,128)(2,1)}) fusion(bf16[3,32,512,128]{3,2,1,0:T(8,128)(2,1)} %refs_0_.9), kind=kLoop, calls=%fused_computation.166 | loop fusion | bytes 18874368 | tf_op jit(solution)/shard_map/slice | solution.py:267
  11.6 8.4 %select_reduce_fusion = f32[3,32,256]{2,1,0:T(8,128)S(1)} fusion(f32[256]{0:T(256)S(1)} %copy-done.13, s32[3,32,256]{2,1,0:T(8,128)S(1)} %pad_add_fusion), kind=kLoop, calls=%fused_computation | loop fusion | flops 18849792 | bytes 197632 | tf_op jit(solution)/shard_map/reduce_sum | solution.py:26
  26.4 4.7 fusion.42
  31.1 28.5 %shard_map.84.refs_6_ = bf16[1,32,128,512]{3,2,1,0:T(8,128)(2,1)} custom-call(bf16[3,32,512,128]{3,2,1,0:T(8,128)(2,1)} %refs_0_.9, f32[3,8,4,2048]{3,2,1,0:T(4,128)} %reshape.933.w_ref, bf16[512,2048]{1,0:T(8,128)(2,1)} %bitcast.44, bf16[2048,512]{1,0:T(8,128)(2,1)} %pad_maximum_fusion.ff_ref), custom_call_target="tpu_custom_call" | custom-call | flops 17179869184 | bytes 8388608 | tf_op jit(solution)/shard_map/pallas_call | solution.py:87
  59.7 20.9 %collective-permute-done.11.refs_2_ = bf16[3,32,128,128]{3,2,1,0:T(8,128)(2,1)} collective-permute-done((bf16[3,32,128,128]{3,2,1,0:T(8,128)(2,1)}, bf16[3,32,128,128]{3,2,1,0:T(8,128)(2,1)}, u32[]{:S(2)}, u32[]{:S(2)}) %collective-permute-start.11) | collective-permute-done | bytes 3145760 | tf_op jit(solution)/shard_map/ppermute | solution.py:214
  82.5 28.5 %shard_map.83.refs_5_ = bf16[1,32,128,512]{3,2,1,0:T(8,128)(2,1)} custom-call(bf16[3,32,512,128]{3,2,1,0:T(8,128)(2,1)} %refs_0_.9, f32[3,8,4,2048]{3,2,1,0:T(4,128)} %reshape.933.w_ref, bf16[512,2048]{1,0:T(8,128)(2,1)} %bitcast.45, bf16[2048,512]{1,0:T(8,128)(2,1)} %pad_maximum_fusion.ff_ref), custom_call_target="tpu_custom_call" | custom-call | flops 17179869184 | bytes 8388608 | tf_op jit(solution)/shard_map/pallas_call | solution.py:87
  111.0 70.4 %collective-permute-done.13.refs_2_ = bf16[3,32,64,128]{3,2,1,0:T(8,128)(2,1)} collective-permute-done((bf16[3,32,64,128]{3,2,1,0:T(8,128)(2,1)}, bf16[3,32,64,128]{3,2,1,0:T(8,128)(2,1)}, u32[]{:S(2)}, u32[]{:S(2)}) %collective-permute-start.13) | collective-permute-done | bytes 1572896 | tf_op jit(solution)/shard_map/ppermute | solution.py:214
  187.7 4.3 copy.50
  192.0 5.1 %reshape.934.refs_7_ = bf16[256,512]{1,0:T(8,128)(2,1)} reshape(bf16[16,16,32,16]{3,2,1,0:T(8,128)(2,1)} %copy.50) | data formatting | bytes 524288 | tf_op jit(solution)/shard_map/reshape | solution.py:293
  197.1 28.4 %shard_map.82.refs_4_ = bf16[1,32,128,512]{3,2,1,0:T(8,128)(2,1)} custom-call(bf16[3,32,512,128]{3,2,1,0:T(8,128)(2,1)} %refs_0_.9, f32[3,8,4,2048]{3,2,1,0:T(4,128)} %reshape.933.w_ref, bf16[512,2048]{1,0:T(8,128)(2,1)} %bitcast.46, bf16[2048,512]{1,0:T(8,128)(2,1)} %pad_maximum_fusion.ff_ref), custom_call_target="tpu_custom_call" | custom-call | flops 17179869184 | bytes 8388608 | tf_op jit(solution)/shard_map/pallas_call | solution.py:87
  225.6 14.7 %shard_map.86 = (bf16[3,32,64,128]{3,2,1,0:T(8,128)(2,1)}, bf16[3,16,64,128]{3,2,1,0:T(8,128)(2,1)}) custom-call(bf16[3,32,512,128]{3,2,1,0:T(8,128)(2,1)} %refs_0_.9, bf16[3,32,64,128]{3,2,1,0:T(8,128)(2,1)} %collective-permute-done.12.refs_1_, bf16[3,32,64,128]{3,2,1,0:T(8,128)(2,1)} %collective-permute-done.13.refs_2_, ...), custom_call_target="tpu_custom_call" | custom-call | flops 3221225472 | bytes 20447232 | tf_op jit(solution)/shard_map/pallas_call | solution.py:148
  243.0 16.3 %shard_map.88 = (bf16[3,32,128,128]{3,2,1,0:T(8,128)(2,1)}, bf16[3,16,128,128]{3,2,1,0:T(8,128)(2,1)}) custom-call(bf16[3,32,512,128]{3,2,1,0:T(8,128)(2,1)} %refs_0_.9, bf16[3,32,128,128]{3,2,1,0:T(8,128)(2,1)} %collective-permute-done.29.refs_1_, bf16[3,32,128,128]{3,2,1,0:T(8,128)(2,1)} %collective-permute-done.11.refs_2_, ...), custom_call_target="tpu_custom_call" | custom-call | flops 6442450944 | bytes 28311552 | tf_op jit(solution)/shard_map/pallas_call | solution.py:148
  265.4 16.4 %shard_map.89 = (bf16[3,32,128,128]{3,2,1,0:T(8,128)(2,1)}, bf16[3,16,128,128]{3,2,1,0:T(8,128)(2,1)}) custom-call(bf16[3,32,512,128]{3,2,1,0:T(8,128)(2,1)} %refs_0_.9, bf16[3,32,128,128]{3,2,1,0:T(8,128)(2,1)} %collective-permute-done.37.refs_1_, bf16[3,32,128,128]{3,2,1,0:T(8,128)(2,1)} %collective-permute-done.refs_2_, ...), custom_call_target="tpu_custom_call" | custom-call | flops 6442450944 | bytes 28311552 | tf_op jit(solution)/shard_map/pallas_call | solution.py:148
  286.8 3.9 collective-permute-done.17
  293.8 16.4 %collective-permute-done.39 = bf16[3,16,64,128]{3,2,1,0:T(8,128)(2,1)S(1)} collective-permute-done((bf16[3,16,64,128]{3,2,1,0:T(8,128)(2,1)S(1)}, bf16[3,16,64,128]{3,2,1,0:T(8,128)(2,1)S(1)}, u32[]{:S(2)}, u32[]{:S(2)}) %collective-permute-start.39) | collective-permute-done | bytes 786464 | tf_op jit(solution)/shard_map/ppermute | solution.py:214
  312.7 9.5 %collective-permute-done.32 = bf16[3,16,32,128]{3,2,1,0:T(8,128)(2,1)S(1)} collective-permute-done((bf16[3,16,32,128]{3,2,1,0:T(8,128)(2,1)S(1)}, bf16[3,16,32,128]{3,2,1,0:T(8,128)(2,1)S(1)}, u32[]{:S(2)}, u32[]{:S(2)}) %collective-permute-start.32) | collective-permute-done | bytes 393248 | tf_op jit(solution)/shard_map/ppermute | solution.py:214
  322.4 6.4 %collective-permute-done.40 = bf16[3,16,32,128]{3,2,1,0:T(8,128)(2,1)S(1)} collective-permute-done((bf16[3,16,32,128]{3,2,1,0:T(8,128)(2,1)S(1)}, bf16[3,16,32,128]{3,2,1,0:T(8,128)(2,1)S(1)}, u32[]{:S(2)}, u32[]{:S(2)}) %collective-permute-start.40) | collective-permute-done | bytes 393248 | tf_op jit(solution)/shard_map/ppermute | solution.py:214
  329.0 10.0 %collective-permute-done.33 = bf16[3,16,16,128]{3,2,1,0:T(8,128)(2,1)S(1)} collective-permute-done((bf16[3,16,16,128]{3,2,1,0:T(8,128)(2,1)S(1)}, bf16[3,16,16,128]{3,2,1,0:T(8,128)(2,1)S(1)}, u32[]{:S(2)}, u32[]{:S(2)}) %collective-permute-start.33) | collective-permute-done | bytes 196640 | tf_op jit(solution)/shard_map/ppermute | solution.py:214
  340.4 7.0 %collective-permute-done.41 = bf16[3,16,16,128]{3,2,1,0:T(8,128)(2,1)S(1)} collective-permute-done((bf16[3,16,16,128]{3,2,1,0:T(8,128)(2,1)S(1)}, bf16[3,16,16,128]{3,2,1,0:T(8,128)(2,1)S(1)}, u32[]{:S(2)}, u32[]{:S(2)}) %collective-permute-start.41) | collective-permute-done | bytes 196640 | tf_op jit(solution)/shard_map/ppermute | solution.py:214
  352.1 16.3 %shard_map.87 = (bf16[3,32,128,128]{3,2,1,0:T(8,128)(2,1)}, bf16[3,16,128,128]{3,2,1,0:T(8,128)(2,1)}) custom-call(bf16[3,32,512,128]{3,2,1,0:T(8,128)(2,1)} %refs_0_.9, bf16[3,32,128,128]{3,2,1,0:T(8,128)(2,1)} %collective-permute-done.21.refs_1_, bf16[3,32,128,128]{3,2,1,0:T(8,128)(2,1)} %collective-permute-done.1.refs_2_, ...), custom_call_target="tpu_custom_call" | custom-call | flops 6442450944 | bytes 28311552 | tf_op jit(solution)/shard_map/pallas_call | solution.py:148
  378.0 14.8 %shard_map.85 = (bf16[3,32,64,128]{3,2,1,0:T(8,128)(2,1)}, bf16[3,16,64,128]{3,2,1,0:T(8,128)(2,1)}) custom-call(bf16[3,32,512,128]{3,2,1,0:T(8,128)(2,1)} %refs_0_.9, bf16[3,32,64,128]{3,2,1,0:T(8,128)(2,1)} %collective-permute-done.2.refs_1_, bf16[3,32,64,128]{3,2,1,0:T(8,128)(2,1)} %copy-done.2, bf16[3,32,64,128]{3,2,1,0:T(8,128)(2,1)} %collective-permute-done.4.refs_3_, ...), custom_call_target="tpu_custom_call" | custom-call | flops 3221225472 | bytes 20447232 | tf_op jit(solution)/shard_map/pallas_call | solution.py:148
  399.6 8.0 %collective-permute-done.5 = bf16[3,16,32,128]{3,2,1,0:T(8,128)(2,1)S(1)} collective-permute-done((bf16[3,16,32,128]{3,2,1,0:T(8,128)(2,1)S(1)}, bf16[3,16,32,128]{3,2,1,0:T(8,128)(2,1)S(1)}, u32[]{:S(2)}, u32[]{:S(2)}) %collective-permute-start.5) | collective-permute-done | bytes 393248 | tf_op jit(solution)/shard_map/ppermute | solution.py:214
  411.0 5.6 %collective-permute-done.6 = bf16[3,16,16,128]{3,2,1,0:T(8,128)(2,1)S(1)} collective-permute-done((bf16[3,16,16,128]{3,2,1,0:T(8,128)(2,1)S(1)}, bf16[3,16,16,128]{3,2,1,0:T(8,128)(2,1)S(1)}, u32[]{:S(2)}, u32[]{:S(2)}) %collective-permute-start.6) | collective-permute-done | bytes 196640 | tf_op jit(solution)/shard_map/ppermute | solution.py:214
  424.3 7.9 %collective-permute-done.26 = bf16[3,16,16,128]{3,2,1,0:T(8,128)(2,1)S(1)} collective-permute-done((bf16[3,16,16,128]{3,2,1,0:T(8,128)(2,1)S(1)}, bf16[3,16,16,128]{3,2,1,0:T(8,128)(2,1)S(1)}, u32[]{:S(2)}, u32[]{:S(2)}) %collective-permute-start.26) | collective-permute-done | bytes 196640 | tf_op jit(solution)/shard_map/ppermute | solution.py:214
  443.1 3.8 collective-permute-start.9
  456.6 7.4 %shard_map.90.refs_3_ = f32[3,32,512,128]{3,2,1,0:T(8,128)} custom-call(bf16[3,32,128,128]{3,2,1,0:T(8,128)(2,1)} %get-tuple-element.35.refs_0_, bf16[3,16,128,128]{3,2,1,0:T(8,128)(2,1)} %maximum_select_fusion.2.refs_1_, bf16[512,256]{1,0:T(8,128)(2,1)} %reshape.938.refs_2_), custom_call_target="tpu_custom_call" | custom-call | flops 805306368 | bytes 9437184 | tf_op jit(solution)/shard_map/pallas_call | solution.py:192
  464.0 3.7 maximum_select_fusion.1.refs_1_
  467.8 7.4 %shard_map.91.refs_3_ = f32[3,32,512,128]{3,2,1,0:T(8,128)} custom-call(bf16[3,32,128,128]{3,2,1,0:T(8,128)(2,1)} %get-tuple-element.32.refs_0_, bf16[3,16,128,128]{3,2,1,0:T(8,128)(2,1)} %maximum_select_fusion.1.refs_1_, bf16[512,256]{1,0:T(8,128)(2,1)} %reshape.938.refs_2_, f32[3,32,512,128]{3,2,1,0:T(8,128)} %shard_map.90.refs_3_), custom_call_target="tpu_custom_call", output_to_operand_aliasing={{}: (3, {})} | custom-call | flops 805306368 | bytes 9437184 | tf_op jit(solution)/shard_map/pallas_call | solution.py:192
  475.2 5.8 %collective-permute-done.10 = bf16[3,16,32,128]{3,2,1,0:T(8,128)(2,1)S(1)} collective-permute-done((bf16[3,16,32,128]{3,2,1,0:T(8,128)(2,1)S(1)}, bf16[3,16,32,128]{3,2,1,0:T(8,128)(2,1)S(1)}, u32[]{:S(2)}, u32[]{:S(2)}) %collective-permute-start.10) | collective-permute-done | bytes 393248 | tf_op jit(solution)/shard_map/ppermute | solution.py:214
  483.9 7.4 %shard_map.92.refs_3_ = f32[3,32,512,128]{3,2,1,0:T(8,128)} custom-call(bf16[3,32,128,128]{3,2,1,0:T(8,128)(2,1)} %get-tuple-element.29.refs_0_, bf16[3,16,128,128]{3,2,1,0:T(8,128)(2,1)} %maximum_select_fusion.refs_1_, bf16[512,256]{1,0:T(8,128)(2,1)} %reshape.938.refs_2_, f32[3,32,512,128]{3,2,1,0:T(8,128)} %shard_map.91.refs_3_), custom_call_target="tpu_custom_call", output_to_operand_aliasing={{}: (3, {})} | custom-call | flops 805306368 | bytes 9437184 | tf_op jit(solution)/shard_map/pallas_call | solution.py:192
  491.4 4.8 shard_map.93.refs_3_
  496.1 4.8 shard_map.94
  (193 shorter events, 94.3 us)
Async XLA Ops:
  8.3 233.1 %collective-permute-start.29 = (bf16[3,32,128,128]{3,2,1,0:T(8,128)(2,1)}, bf16[3,32,128,128]{3,2,1,0:T(8,128)(2,1)}, u32[]{:S(2)}, u32[]{:S(2)}) collective-permute-start(bf16[3,32,128,128]{3,2,1,0:T(8,128)(2,1)} %get-tuple-element.37), channel_id=1, source_target_pairs={{0,1},{1,0},{2,3},{3,2},{4,5},{5,4},{6,7},{7,6},{8,9},{9,8},{10,11... | collective-permute-start | bytes 9437192 | tf_op jit(solution)/shard_map/ppermute | solution.py:214
  8.7 71.8 %collective-permute-start.11 = (bf16[3,32,128,128]{3,2,1,0:T(8,128)(2,1)}, bf16[3,32,128,128]{3,2,1,0:T(8,128)(2,1)}, u32[]{:S(2)}, u32[]{:S(2)}) collective-permute-start(bf16[3,32,128,128]{3,2,1,0:T(8,128)(2,1)} %get-tuple-element.37), channel_id=1, source_target_pairs={{0,2},{1,3},{2,0},{3,1},{4,6},{5,7},{6,4},{7,5},{8,10},{9,11},{10,... | collective-permute-start | bytes 9437192 | tf_op jit(solution)/shard_map/ppermute | solution.py:214
  11.3 172.0 %collective-permute-start = (bf16[3,32,128,128]{3,2,1,0:T(8,128)(2,1)}, bf16[3,32,128,128]{3,2,1,0:T(8,128)(2,1)}, u32[]{:S(2)}, u32[]{:S(2)}) collective-permute-start(bf16[3,32,128,128]{3,2,1,0:T(8,128)(2,1)} %get-tuple-element.38), channel_id=1, source_target_pairs={{0,2},{1,3},{2,0},{3,1},{4,6},{5,7},{6,4},{7,5},{8,10},{9,11},{10,... | collective-permute-start | bytes 9437192 | tf_op jit(solution)/shard_map/ppermute | solution.py:214
  80.6 100.9 %collective-permute-start.13 = (bf16[3,32,64,128]{3,2,1,0:T(8,128)(2,1)}, bf16[3,32,64,128]{3,2,1,0:T(8,128)(2,1)}, u32[]{:S(2)}, u32[]{:S(2)}) collective-permute-start(bf16[3,32,64,128]{3,2,1,0:T(8,128)(2,1)} %get-tuple-element.25), channel_id=1, source_target_pairs={{0,2},{1,3},{2,0},{3,1},{4,6},{5,7},{6,4},{7,5},{8,10},{9,11},{10,... | collective-permute-start | bytes 4718600 | tf_op jit(solution)/shard_map/ppermute | solution.py:214
  111.0 75.7 %collective-permute-start.12 = (bf16[3,32,64,128]{3,2,1,0:T(8,128)(2,1)}, bf16[3,32,64,128]{3,2,1,0:T(8,128)(2,1)}, u32[]{:S(2)}, u32[]{:S(2)}) collective-permute-start(bf16[3,32,64,128]{3,2,1,0:T(8,128)(2,1)} %get-tuple-element.25), channel_id=1, source_target_pairs={{0,1},{1,0},{2,3},{3,2},{4,5},{5,4},{6,7},{7,6},{8,9},{9,8},{10,11... | collective-permute-start | bytes 4718600 | tf_op jit(solution)/shard_map/ppermute | solution.py:214
  182.3 59.2 %collective-permute-start.30 = (bf16[3,32,128,128]{3,2,1,0:T(8,128)(2,1)}, bf16[3,32,128,128]{3,2,1,0:T(8,128)(2,1)}, u32[]{:S(2)}, u32[]{:S(2)}) collective-permute-start(bf16[3,32,128,128]{3,2,1,0:T(8,128)(2,1)} %collective-permute-done.11.refs_2_), channel_id=1, source_target_pairs={{0,1},{1,0},{2,3},{3,2},{4,5},{5,4},{6,7},{7,6},{8,9},{9,8},{10,11... | collective-permute-start | bytes 9437192 | tf_op jit(solution)/shard_map/ppermute | solution.py:214
  183.3 78.2 %collective-permute-start.1 = (bf16[3,32,128,128]{3,2,1,0:T(8,128)(2,1)}, bf16[3,32,128,128]{3,2,1,0:T(8,128)(2,1)}, u32[]{:S(2)}, u32[]{:S(2)}) collective-permute-start(bf16[3,32,128,128]{3,2,1,0:T(8,128)(2,1)} %get-tuple-element.21), channel_id=1, source_target_pairs={{0,2},{1,3},{2,0},{3,1},{4,6},{5,7},{6,4},{7,5},{8,10},{9,11},{10,... | collective-permute-start | bytes 9437192 | tf_op jit(solution)/shard_map/ppermute | solution.py:214
  186.7 76.7 %collective-permute-start.37 = (bf16[3,32,128,128]{3,2,1,0:T(8,128)(2,1)}, bf16[3,32,128,128]{3,2,1,0:T(8,128)(2,1)}, u32[]{:S(2)}, u32[]{:S(2)}) collective-permute-start(bf16[3,32,128,128]{3,2,1,0:T(8,128)(2,1)} %get-tuple-element.38), channel_id=1, source_target_pairs={{0,1},{1,0},{2,3},{3,2},{4,5},{5,4},{6,7},{7,6},{8,9},{9,8},{10,11... | collective-permute-start | bytes 9437192 | tf_op jit(solution)/shard_map/ppermute | solution.py:214
  186.8 76.8 %collective-permute-start.38 = (bf16[3,32,128,128]{3,2,1,0:T(8,128)(2,1)}, bf16[3,32,128,128]{3,2,1,0:T(8,128)(2,1)}, u32[]{:S(2)}, u32[]{:S(2)}) collective-permute-start(bf16[3,32,128,128]{3,2,1,0:T(8,128)(2,1)} %collective-permute-done.refs_2_), channel_id=1, source_target_pairs={{0,1},{1,0},{2,3},{3,2},{4,5},{5,4},{6,7},{7,6},{8,9},{9,8},{10,11... | collective-permute-start | bytes 9437192 | tf_op jit(solution)/shard_map/ppermute | solution.py:214
  241.4 107.6 %collective-permute-start.21 = (bf16[3,32,128,128]{3,2,1,0:T(8,128)(2,1)S(1)}, bf16[3,32,128,128]{3,2,1,0:T(8,128)(2,1)}, u32[]{:S(2)}, u32[]{:S(2)}) collective-permute-start(bf16[3,32,128,128]{3,2,1,0:T(8,128)(2,1)S(1)} %copy-done.1), channel_id=1, source_target_pairs={{0,1},{1,0},{2,3},{3,2},{4,5},{5,4},{6,7},{7,6},{8,9},{9,8},{10,11... | collective-permute-start | bytes 9437192 | tf_op jit(solution)/shard_map/ppermute | solution.py:214
  241.5 20.5 %collective-permute-start.15 = (bf16[3,16,32,128]{3,2,1,0:T(8,128)(2,1)S(1)}, bf16[3,16,32,128]{3,2,1,0:T(8,128)(2,1)}, u32[]{:S(2)}, u32[]{:S(2)}) collective-permute-start(bf16[3,16,32,128]{3,2,1,0:T(8,128)(2,1)S(1)} %constant_dynamic-slice_fusion.11), channel_id=1, source_target_pairs={{0,4},{4,0},{8,12},{12,8},{16,20},{20,16},{24,28},{28,24},{1,5},{5... | collective-permute-start | bytes 1179656 | tf_op jit(solution)/shard_map/ppermute | solution.py:214
  261.5 31.2 %collective-permute-start.31 = (bf16[3,16,64,128]{3,2,1,0:T(8,128)(2,1)}, bf16[3,16,64,128]{3,2,1,0:T(8,128)(2,1)S(1)}, u32[]{:S(2)}, u32[]{:S(2)}) collective-permute-start(bf16[3,16,64,128]{3,2,1,0:T(8,128)(2,1)} %constant_dynamic-slice_fusion.5), channel_id=1, source_target_pairs={{0,4},{4,0},{8,12},{12,8},{16,20},{20,16},{24,28},{28,24},{1,5},{5... | collective-permute-start | bytes 2359304 | tf_op jit(solution)/shard_map/ppermute | solution.py:214
  262.0 85.5 %collective-permute-start.3 = (bf16[3,32,64,128]{3,2,1,0:T(8,128)(2,1)}, bf16[3,32,64,128]{3,2,1,0:T(8,128)(2,1)S(1)}, u32[]{:S(2)}, u32[]{:S(2)}) collective-permute-start(bf16[3,32,64,128]{3,2,1,0:T(8,128)(2,1)} %get-tuple-element.22), channel_id=1, source_target_pairs={{0,2},{1,3},{2,0},{3,1},{4,6},{5,7},{6,4},{7,5},{8,10},{9,11},{10,... | collective-permute-start | bytes 4718600 | tf_op jit(solution)/shard_map/ppermute | solution.py:214
  263.5 88.6 %collective-permute-start.22 = (bf16[3,32,128,128]{3,2,1,0:T(8,128)(2,1)}, bf16[3,32,128,128]{3,2,1,0:T(8,128)(2,1)}, u32[]{:S(2)}, u32[]{:S(2)}) collective-permute-start(bf16[3,32,128,128]{3,2,1,0:T(8,128)(2,1)} %collective-permute-done.1.refs_2_), channel_id=1, source_target_pairs={{0,1},{1,0},{2,3},{3,2},{4,5},{5,4},{6,7},{7,6},{8,9},{9,8},{10,11... | collective-permute-start | bytes 9437192 | tf_op jit(solution)/shard_map/ppermute | solution.py:214
  263.5 18.3 %collective-permute-start.16 = (bf16[3,16,16,128]{3,2,1,0:T(8,128)(2,1)S(1)}, bf16[3,16,16,128]{3,2,1,0:T(8,128)(2,1)}, u32[]{:S(2)}, u32[]{:S(2)}) collective-permute-start(bf16[3,16,16,128]{3,2,1,0:T(8,128)(2,1)S(1)} %constant_dynamic-slice_fusion.10), channel_id=1, source_target_pairs={{0,8},{4,12},{8,0},{12,4},{16,24},{20,28},{24,16},{28,20},{1,9},{5... | collective-permute-start | bytes 589832 | tf_op jit(solution)/shard_map/ppermute | solution.py:214
  290.7 19.5 %collective-permute-start.39 = (bf16[3,16,64,128]{3,2,1,0:T(8,128)(2,1)S(1)}, bf16[3,16,64,128]{3,2,1,0:T(8,128)(2,1)S(1)}, u32[]{:S(2)}, u32[]{:S(2)}) collective-permute-start(bf16[3,16,64,128]{3,2,1,0:T(8,128)(2,1)S(1)} %constant_dynamic-slice_fusion.2), channel_id=1, source_target_pairs={{0,4},{4,0},{8,12},{12,8},{16,20},{20,16},{24,28},{28,24},{1,5},{5... | collective-permute-start | bytes 2359304 | tf_op jit(solution)/shard_map/ppermute | solution.py:214
  292.7 17.9 %collective-permute-start.18 = (bf16[3,16,8,128]{3,2,1,0:T(8,128)(2,1)S(1)}, bf16[3,16,8,128]{3,2,1,0:T(8,128)(2,1)S(1)}, u32[]{:S(2)}, u32[]{:S(2)}) collective-permute-start(bf16[3,16,8,128]{3,2,1,0:T(8,128)(2,1)S(1)} %bitcast.54), channel_id=1, source_target_pairs={{0,16},{4,20},{8,24},{12,28},{16,0},{20,4},{24,8},{28,12},{1,17},{... | collective-permute-start | bytes 294920 | tf_op jit(solution)/shard_map/ppermute | solution.py:214
  310.6 18.3 %collective-permute-start.40 = (bf16[3,16,32,128]{3,2,1,0:T(8,128)(2,1)S(1)}, bf16[3,16,32,128]{3,2,1,0:T(8,128)(2,1)S(1)}, u32[]{:S(2)}, u32[]{:S(2)}) collective-permute-start(bf16[3,16,32,128]{3,2,1,0:T(8,128)(2,1)S(1)} %constant_dynamic-slice_fusion.1), channel_id=1, source_target_pairs={{0,8},{4,12},{8,0},{12,4},{16,24},{20,28},{24,16},{28,20},{1,9},{5... | collective-permute-start | bytes 1179656 | tf_op jit(solution)/shard_map/ppermute | solution.py:214
  322.3 55.4 %collective-permute-start.2 = (bf16[3,32,64,128]{3,2,1,0:T(8,128)(2,1)}, bf16[3,32,64,128]{3,2,1,0:T(8,128)(2,1)}, u32[]{:S(2)}, u32[]{:S(2)}) collective-permute-start(bf16[3,32,64,128]{3,2,1,0:T(8,128)(2,1)} %get-tuple-element.22), channel_id=1, source_target_pairs={{0,1},{1,0},{2,3},{3,2},{4,5},{5,4},{6,7},{7,6},{8,9},{9,8},{10,11... | collective-permute-start | bytes 4718600 | tf_op jit(solution)/shard_map/ppermute | solution.py:214
  347.5 22.2 %collective-permute-start.19 = (bf16[3,16,16,128]{3,2,1,0:T(8,128)(2,1)S(1)}, bf16[3,16,16,128]{3,2,1,0:T(8,128)(2,1)S(1)}, u32[]{:S(2)}, u32[]{:S(2)}) collective-permute-start(bf16[3,16,16,128]{3,2,1,0:T(8,128)(2,1)S(1)} %maximum_select_fusion.14), channel_id=1, source_target_pairs={{0,8},{4,12},{8,0},{12,4},{16,24},{20,28},{24,16},{28,20},{1,9},{5... | collective-permute-start | bytes 589832 | tf_op jit(solution)/shard_map/ppermute | solution.py:214
  347.5 30.6 %collective-permute-start.4 = (bf16[3,32,64,128]{3,2,1,0:T(8,128)(2,1)S(1)}, bf16[3,32,64,128]{3,2,1,0:T(8,128)(2,1)}, u32[]{:S(2)}, u32[]{:S(2)}) collective-permute-start(bf16[3,32,64,128]{3,2,1,0:T(8,128)(2,1)S(1)} %collective-permute-done.3.refs_2_), channel_id=1, source_target_pairs={{0,1},{1,0},{2,3},{3,2},{4,5},{5,4},{6,7},{7,6},{8,9},{9,8},{10,11... | collective-permute-start | bytes 4718600 | tf_op jit(solution)/shard_map/ppermute | solution.py:214
  348.9 24.1 %collective-permute-start.34 = (bf16[3,16,16,128]{3,2,1,0:T(8,128)(2,1)}, bf16[3,16,16,128]{3,2,1,0:T(8,128)(2,1)S(1)}, u32[]{:S(2)}, u32[]{:S(2)}) collective-permute-start(bf16[3,16,16,128]{3,2,1,0:T(8,128)(2,1)} %bitcast.19), channel_id=1, source_target_pairs={{0,16},{4,20},{8,24},{12,28},{16,0},{20,4},{24,8},{28,12},{1,17},{... | collective-permute-start | bytes 589832 | tf_op jit(solution)/shard_map/ppermute | solution.py:214
  352.0 22.7 %collective-permute-start.42 = (bf16[3,16,16,128]{3,2,1,0:T(8,128)(2,1)}, bf16[3,16,16,128]{3,2,1,0:T(8,128)(2,1)S(1)}, u32[]{:S(2)}, u32[]{:S(2)}) collective-permute-start(bf16[3,16,16,128]{3,2,1,0:T(8,128)(2,1)} %bitcast.21), channel_id=1, source_target_pairs={{0,16},{4,20},{8,24},{12,28},{16,0},{20,4},{24,8},{28,12},{1,17},{... | collective-permute-start | bytes 589832 | tf_op jit(solution)/shard_map/ppermute | solution.py:214
  370.3 25.1 %collective-permute-start.23 = (bf16[3,16,64,128]{3,2,1,0:T(8,128)(2,1)S(1)}, bf16[3,16,64,128]{3,2,1,0:T(8,128)(2,1)S(1)}, u32[]{:S(2)}, u32[]{:S(2)}) collective-permute-start(bf16[3,16,64,128]{3,2,1,0:T(8,128)(2,1)S(1)} %constant_dynamic-slice_fusion.8), channel_id=1, source_target_pairs={{0,4},{4,0},{8,12},{12,8},{16,20},{20,16},{24,28},{28,24},{1,5},{5... | collective-permute-start | bytes 2359304 | tf_op jit(solution)/shard_map/ppermute | solution.py:214
  373.0 77.4 %collective-permute-start.20 = (bf16[3,16,32,128]{3,2,1,0:T(8,128)(2,1)S(1)}, bf16[3,16,32,128]{3,2,1,0:T(8,128)(2,1)}, u32[]{:S(2)}, u32[]{:S(2)}) collective-permute-start(bf16[3,16,32,128]{3,2,1,0:T(8,128)(2,1)S(1)} %maximum_select_fusion.9), channel_id=1, source_target_pairs={{0,4},{4,0},{8,12},{12,8},{16,20},{20,16},{24,28},{28,24},{1,5},{5... | collective-permute-start | bytes 1179656 | tf_op jit(solution)/shard_map/ppermute | solution.py:214
  374.7 61.9 %collective-permute-start.35 = (bf16[3,16,32,128]{3,2,1,0:T(8,128)(2,1)S(1)}, bf16[3,16,32,128]{3,2,1,0:T(8,128)(2,1)}, u32[]{:S(2)}, u32[]{:S(2)}) collective-permute-start(bf16[3,16,32,128]{3,2,1,0:T(8,128)(2,1)S(1)} %maximum_select_fusion.11), channel_id=1, source_target_pairs={{0,8},{4,12},{8,0},{12,4},{16,24},{20,28},{24,16},{28,20},{1,9},{5... | collective-permute-start | bytes 1179656 | tf_op jit(solution)/shard_map/ppermute | solution.py:214
  377.6 20.0 %collective-permute-start.43 = (bf16[3,16,32,128]{3,2,1,0:T(8,128)(2,1)S(1)}, bf16[3,16,32,128]{3,2,1,0:T(8,128)(2,1)}, u32[]{:S(2)}, u32[]{:S(2)}) collective-permute-start(bf16[3,16,32,128]{3,2,1,0:T(8,128)(2,1)S(1)} %maximum_select_fusion.12), channel_id=1, source_target_pairs={{0,8},{4,12},{8,0},{12,4},{16,24},{20,28},{24,16},{28,20},{1,9},{5... | collective-permute-start | bytes 1179656 | tf_op jit(solution)/shard_map/ppermute | solution.py:214
  399.0 54.4 %collective-permute-start.44 = (bf16[3,16,64,128]{3,2,1,0:T(8,128)(2,1)S(1)}, bf16[3,16,64,128]{3,2,1,0:T(8,128)(2,1)}, u32[]{:S(2)}, u32[]{:S(2)}) collective-permute-start(bf16[3,16,64,128]{3,2,1,0:T(8,128)(2,1)S(1)} %maximum_select_fusion.7), channel_id=1, source_target_pairs={{0,4},{4,0},{8,12},{12,8},{16,20},{20,16},{24,28},{28,24},{1,5},{5... | collective-permute-start | bytes 2359304 | tf_op jit(solution)/shard_map/ppermute | solution.py:214
  433.1 13.9 %collective-permute-start.27 = (bf16[3,16,32,128]{3,2,1,0:T(8,128)(2,1)}, bf16[3,16,32,128]{3,2,1,0:T(8,128)(2,1)}, u32[]{:S(2)}, u32[]{:S(2)}) collective-permute-start(bf16[3,16,32,128]{3,2,1,0:T(8,128)(2,1)} %maximum_select_fusion.10), channel_id=1, source_target_pairs={{0,8},{4,12},{8,0},{12,4},{16,24},{20,28},{24,16},{28,20},{1,9},{5... | collective-permute-start | bytes 1179656 | tf_op jit(solution)/shard_map/ppermute | solution.py:214
  438.9 25.1 %collective-permute-start.36 = (bf16[3,16,64,128]{3,2,1,0:T(8,128)(2,1)}, bf16[3,16,64,128]{3,2,1,0:T(8,128)(2,1)}, u32[]{:S(2)}, u32[]{:S(2)}) collective-permute-start(bf16[3,16,64,128]{3,2,1,0:T(8,128)(2,1)} %maximum_select_fusion.6), channel_id=1, source_target_pairs={{0,4},{4,0},{8,12},{12,8},{16,20},{20,16},{24,28},{28,24},{1,5},{5... | collective-permute-start | bytes 2359304 | tf_op jit(solution)/shard_map/ppermute | solution.py:214
  448.8 33.3 %collective-permute-start.28 = (bf16[3,16,64,128]{3,2,1,0:T(8,128)(2,1)S(1)}, bf16[3,16,64,128]{3,2,1,0:T(8,128)(2,1)S(1)}, u32[]{:S(2)}, u32[]{:S(2)}) collective-permute-start(bf16[3,16,64,128]{3,2,1,0:T(8,128)(2,1)S(1)} %maximum_select_fusion.5), channel_id=1, source_target_pairs={{0,4},{4,0},{8,12},{12,8},{16,20},{20,16},{24,28},{28,24},{1,5},{5... | collective-permute-start | bytes 2359304 | tf_op jit(solution)/shard_map/ppermute | solution.py:214
  452.9 28.1 %collective-permute-start.10 = (bf16[3,16,32,128]{3,2,1,0:T(8,128)(2,1)S(1)}, bf16[3,16,32,128]{3,2,1,0:T(8,128)(2,1)S(1)}, u32[]{:S(2)}, u32[]{:S(2)}) collective-permute-start(bf16[3,16,32,128]{3,2,1,0:T(8,128)(2,1)S(1)} %maximum_select_fusion.8), channel_id=1, source_target_pairs={{0,4},{4,0},{8,12},{12,8},{16,20},{20,16},{24,28},{28,24},{1,5},{5... | collective-permute-start | bytes 1179656 | tf_op jit(solution)/shard_map/ppermute | solution.py:214
  (28 other events, 605.1 us)
